TPU v7x, 128 devices: a whole 4x4x4 slice. The times are simulated.
128 devices in a mesh: mem: 4 (over x_lo, core), lat: 32 (over x_hi, z, y).
Axes of the slice: x: 4 (x_hi: 2, x_lo: 2; x = x_hi * 2 + x_lo), y: 4, z: 4, core: 2. Of those that a mesh axis runs over, the one named last changes fastest.
Arguments:
- latent: bfloat16 [8, 16384, 1024], P('mem', 'lat'), may hold values from -8 to 8
- member_noise: bfloat16 [8, 1024], P('mem'), may hold values from -3 to 3
- w_qkv: bfloat16 [1024, 3072], replicated, may hold values from -0.28125 to 0.28125
- w_out: bfloat16 [1024, 1024], replicated, may hold values from -0.1875 to 0.1875
- dec_weight: bfloat16 [100, 1024], replicated, may hold values from -0.1875 to 0.1875
- targets: float32 [100, 16384], P(None, 'lat'), may hold values from -6 to 6
- area_weight: float32 [16384], P('lat'), may hold values from 0.1 to 1
- field_weight: float32 [100], replicated, may hold values from 0.2 to 2
- band_count: int32 [32], replicated, may hold values from 192 to 512, as said below
- band_window: int32 [32, 2], P('lat'), may hold values from 128 to 256
Outputs:
- grad_hidden: bfloat16 [8, 16384, 1024], P('mem', 'lat')
- grad_dec_weight: float32 [100, 1024], replicated
- mean_loss: float32 [], replicated
Inputs may be any that keep to these rules, and one draw needn't show every extreme that they name: 512 at the first band and at the middle band; the other bands vary and tend to hold fewer the farther they lie from the middle, without falling in order; rows at band_count[b] and above of band b are unused slots.
All inputs are finite; a program needn't handle non-finite values.
Results may differ from a plain program's by a relative error of at most 0.015.
Values may be sent and summed in bfloat16 or wider, within the bound.
No kernel may reach another device: no remote copies, remote signals or barrier semaphores. Data moves between devices by JAX's collectives and lax.ppermute only.
A program may use at most 192 MiB of HBM per device.

v0:
```python
import functools

import jax
import jax.numpy as jnp
from jax import lax
from jax.experimental import pallas as pl
from jax.experimental.pallas import tpu as pltpu
from jax.sharding import PartitionSpec as P

HEAD_DIM = 64
HALO = 256
LOG2E = 1.4426950408889634

norm_eps = 1e-05
smooth_width = 0.25
F32 = jnp.float32
BF16 = jnp.bfloat16
MIB = 1024 * 1024


def normalize(x):
    mean = jnp.mean(x, axis=-1, keepdims=True)
    centred = x - mean
    var = jnp.mean(centred * centred, axis=-1, keepdims=True)
    inverse = lax.rsqrt(var + norm_eps)
    return centred * inverse, inverse


def nt_dot(a, b):
    return lax.dot_general(a, b, (((1,), (1,)), ((), ())), preferred_element_type=F32)


def tn_dot(a, b):
    return lax.dot_general(a, b, (((0,), (0,)), ((), ())), preferred_element_type=F32)


def nn_dot(a, b):
    return jnp.dot(a, b, preferred_element_type=F32)


QB = 256
STEP_COLS = 256
PAIR = 2 * HEAD_DIM
FIELD_TILE = 8
LOSS_PIECE = 104
NEVER = -1e30


def bias_of(q_row, k_row, place_ref, count_ref, window_ref, rows):
    bands = count_ref.shape[0]
    band = lax.rem(place_ref[0], bands)
    offset = k_row - q_row
    in_window = (offset >= -window_ref[0, 0]) & (offset <= window_ref[0, 1])
    before = jnp.where(band > 0, count_ref[jnp.maximum(band - 1, 0)], 0)
    after = jnp.where(band < bands - 1, count_ref[jnp.minimum(band + 1, bands - 1)], 0)
    end = jnp.where(
        k_row < 0, before - rows, jnp.where(k_row < rows, count_ref[band], after + rows)
    )
    return jnp.where((in_window & (k_row < end)) | (offset == 0), 0.0, NEVER)


def iota(shape, axis):
    return lax.broadcasted_iota(jnp.int32, shape, axis)


def pair_scores(q, keys, bias, low):
    zero = jnp.zeros_like(q)
    both = jnp.concatenate([jnp.where(low, q, zero), jnp.where(low, zero, q)], axis=0)
    scores = nt_dot(both, keys)
    weights, tops = [], []
    for half in range(2):
        part = scores[half * q.shape[0] : (half + 1) * q.shape[0]] + bias
        top = jnp.max(part, axis=-1, keepdims=True)
        weights.append(jnp.exp2(part - top).astype(BF16))
        tops.append(top)
    return jnp.concatenate(weights, axis=1), jnp.where(low, tops[0], tops[1])


def set_ones(ref, low):
    half = ref.shape[-2] // 2
    one = jnp.ones((half, PAIR), BF16)
    for pair in range(ref.shape[0]):
        for group in range(ref.shape[1]):
            ref[pair, group, :half, PAIR:] = jnp.where(low, one, 0.0).astype(BF16)
            ref[pair, group, half:, PAIR:] = jnp.where(low, 0.0, one).astype(BF16)


def set_values(ref, group, at, value, low):
    half, count = ref.shape[-2] // 2, value.shape[0]
    for pair in range(ref.shape[0]):
        own = value[:, pair * PAIR : (pair + 1) * PAIR]
        zero = jnp.zeros_like(own)
        ref[pair, group, at : at + count, :PAIR] = jnp.where(low, own, zero)
        ref[pair, group, half + at : half + at + count, :PAIR] = jnp.where(low, zero, own)


def near_body(
    place_ref, count_ref, window_ref, latent_ref, wq_ref, wk_ref, wv_ref, q_ref, o_ref, lse_ref, normed_ref, bias_ref, k_ref, vx_ref
):
    step = pl.program_id(0)
    rows = bias_ref.shape[0]
    members = latent_ref.shape[0] // rows
    low = iota((1, PAIR), 1) < HEAD_DIM

    @pl.when(step == 0)
    def _():
        normed_ref[...] = normalize(latent_ref[...].astype(F32))[0].astype(BF16)
        shape = bias_ref.shape
        bias_ref[...] = bias_of(iota(shape, 0), iota(shape, 1), place_ref, count_ref, window_ref, rows)
        set_ones(vx_ref, low)


    def queries(at):
        span = slice(at, at + QB)
        q_ref[span] = (
            nn_dot(normed_ref[span], wq_ref[...]) * (HEAD_DIM ** (-0.5) * LOG2E)
        ).astype(BF16)

    def keys(at):
        span = slice(at, at + QB)
        k_ref[span] = nn_dot(normed_ref[span], wk_ref[...]).astype(BF16)

    def values(at):
        span = slice(at, at + QB)
        value = nn_dot(normed_ref[span], wv_ref[...]).astype(BF16)
        set_values(vx_ref, at // rows, at % rows, value, low)

    def attend(member, pair, block):
        cols = slice(pair * PAIR, (pair + 1) * PAIR)
        here = slice(block * QB, (block + 1) * QB)
        mine = slice(member * rows + block * QB, member * rows + (block + 1) * QB)
        reach = slice(member * rows, (member + 1) * rows)
        weight, top = pair_scores(q_ref[mine, cols], k_ref[reach, cols], bias_ref[here], low)
        total = nn_dot(weight, vx_ref[pair, member])
        summed_weight = total[:, PAIR:]
        o_ref[mine, cols] = (total[:, :PAIR] / summed_weight).astype(BF16)
        lse_ref[mine, cols] = top + jnp.log2(summed_weight)

    pairs, blocks = STEP_COLS // PAIR, rows // QB
    project = [
        [(f, member * rows + at) for f in (keys, values, queries) for at in range(0, rows, QB)]
        for member in range(members)
    ]
    for f, at in project[0]:
        f(at)
    for member in range(members):
        later = project[member + 1] if member + 1 < members else []
        tiles = [(pair, block) for pair in range(pairs) for block in range(blocks)]
        share = -(-len(later) // len(tiles))
        for i, (pair, block) in enumerate(tiles):
            for f, at in later[i * share : (i + 1) * share]:
                f(at)
            attend(member, pair, block)


def near(place, latent, w_qkv):
    members, rows, width = latent.shape
    tall = members * rows
    steps = width // STEP_COLS
    block = pl.BlockSpec((tall, STEP_COLS), lambda s: (0, s))
    return pl.pallas_call(
        near_body,
        grid=(steps,),
        in_specs=[
            *[pl.BlockSpec(memory_space=pltpu.SMEM)] * 3,
            pl.BlockSpec((tall, width), lambda s: (0, 0), pipeline_mode=pl.Buffered(1)),
            pl.BlockSpec((width, STEP_COLS), lambda s: (0, s)),
            pl.BlockSpec((width, STEP_COLS), lambda s: (0, steps + s)),
            pl.BlockSpec((width, STEP_COLS), lambda s: (0, 2 * steps + s)),
        ],
        out_specs=[block, block, block],
        out_shape=[
            jax.ShapeDtypeStruct((tall, width), BF16),
            jax.ShapeDtypeStruct((tall, width), BF16),
            jax.ShapeDtypeStruct((tall, width), F32),
        ],
        scratch_shapes=[
            pltpu.VMEM((tall, width), BF16),
            pltpu.VMEM((rows, rows), F32),
            pltpu.VMEM((tall, STEP_COLS), BF16),
            pltpu.VMEM((STEP_COLS // PAIR, members, 2 * rows, 2 * PAIR), BF16),
        ],
        compiler_params=pltpu.CompilerParams(vmem_limit_bytes=60 * MIB),
        cost_estimate=pl.CostEstimate(
            flops=20 * 10**9, bytes_accessed=16 * MIB, transcendentals=10**7
        ),
        name="near",
    )(*place, latent.reshape(tall, width), w_qkv, w_qkv, w_qkv)


def far_body(
    place_ref,
    count_ref,
    window_ref,
    q_ref,
    o_ref,
    lse_ref,
    before_ref,
    after_ref,
    wk_ref,
    wv_ref,
    noise_ref,
    dec_ref,
    latent_hbm,
    wout_hbm,
    normalized_hbm,
    inverse_ref,
    normed_out_hbm,
    predicted_ref,
    padded_ref,
    halo_ref,
    bias_ref,
    k_ref,
    vx_ref,
    att_ref,
    latent_ref,
    wout_ref,
    normalized_ref,
    normed_out_ref,
    sem,
    out_sem,
):
    step = pl.program_id(0)
    members, _, width = before_ref.shape
    tall = q_ref.shape[0]
    rows = tall // members
    low = iota((1, PAIR), 1) < HEAD_DIM
    late = [
        pltpu.make_async_copy(latent_hbm, latent_ref, sem.at[0]),
        pltpu.make_async_copy(wout_hbm, wout_ref, sem.at[1]),
    ]

    @pl.when(step == 0)
    def _():
        for copy in late:
            copy.start()
        padded_ref[...] = jnp.zeros_like(padded_ref)
        padded_ref[: dec_ref.shape[0]] = dec_ref[...]
        for member in range(members):
            for side, source in enumerate((before_ref, after_ref)):
                at = (2 * member + side) * HALO
                halo_ref[at : at + HALO] = normalize(source[member].astype(F32))[0].astype(BF16)
        shape = (HALO, HALO)
        bias_ref[0] = bias_of(iota(shape, 0), iota(shape, 1) - HALO, place_ref, count_ref, window_ref, rows)
        bias_ref[1] = bias_of(iota(shape, 0) + rows - HALO, iota(shape, 1) + rows, place_ref, count_ref, window_ref, rows)
        set_ones(vx_ref, low)

    def keys(at):
        span = slice(at, at + HALO)
        k_ref[span] = nn_dot(halo_ref[span], wk_ref[...]).astype(BF16)

    def values(at):
        span = slice(at, at + HALO)
        value = nn_dot(halo_ref[span], wv_ref[...]).astype(BF16)
        set_values(vx_ref, at // HALO, 0, value, low)

    def attend(member, pair, side):
        cols = slice(pair * PAIR, (pair + 1) * PAIR)
        out_cols = pl.ds(pl.multiple_of(step * STEP_COLS + pair * PAIR, PAIR), PAIR)
        at = member * rows + side * (rows - HALO)
        mine = slice(at, at + HALO)
        reach = slice((2 * member + side) * HALO, (2 * member + side + 1) * HALO)
        lse = lse_ref[mine, cols]
        weight, far_top = pair_scores(q_ref[mine, cols], k_ref[reach, cols], bias_ref[side], low)
        total = nn_dot(weight, vx_ref[pair, 2 * member + side])
        top = jnp.maximum(lse, far_top)
        near_share, far_share = jnp.exp2(lse - top), jnp.exp2(far_top - top)
        att_ref[mine, out_cols] = (
            (near_share * o_ref[mine, cols].astype(F32) + far_share * total[:, :PAIR])
            / (near_share + far_share * total[:, PAIR:])
        ).astype(BF16)

    groups = [(member, side) for member in range(members) for side in range(2)]

    def project(group):
        keys(group * HALO)
        values(group * HALO)

    project(0)
    for group, (member, side) in enumerate(groups):
        if group + 1 < len(groups):
            project(group + 1)
        for pair in range(STEP_COLS // PAIR):
            attend(member, pair, side)

    @pl.when(step == pl.num_programs(0) - 1)
    def _():
        for copy in late:
            copy.wait()
        copies = []
        chunks = [(member, at) for member in range(members) for at in range(0, rows, HALO)]

        def hidden_of(member, at):
            attended = att_ref[member * rows + at : member * rows + at + HALO]
            return latent_ref[member, at : at + HALO].astype(F32) + nn_dot(attended, wout_ref[...])

        hidden = hidden_of(*chunks[0])
        for index, (member, at) in enumerate(chunks):
            after = hidden_of(*chunks[index + 1]) if index + 1 < len(chunks) else None
            span = slice(at, at + HALO)
            normalized, inverse = normalize(hidden)
            normalized_ref[member, span] = normalized.astype(BF16)
            inverse_ref[member, span] = jnp.broadcast_to(inverse, (HALO, inverse_ref.shape[2]))
            normed_out = (normalized + noise_ref[member : member + 1].astype(F32)).astype(BF16)
            normed_out_ref[member, span] = normed_out
            predicted_ref[member, :, span] = nt_dot(padded_ref[...], normed_out).astype(BF16)
            for source, target in ((normalized_ref, normalized_hbm), (normed_out_ref, normed_out_hbm)):
                copy = pltpu.make_async_copy(
                    source.at[member, span], target.at[member, span], out_sem.at[len(copies)]
                )
                copy.start()
                copies.append(copy)
            hidden = after
        for copy in copies:
            copy.wait()


def far(place, q, o, lse, before, after, w_qkv, noise, dec, latent, w_out):
    members, rows, width = latent.shape
    tall = members * rows
    fields = dec.shape[0]
    padded = -(-fields // FIELD_TILE) * FIELD_TILE
    steps = width // STEP_COLS
    block = pl.BlockSpec((tall, STEP_COLS), lambda s: (0, s))
    whole2 = lambda s: (0, 0)
    whole3 = lambda s: (0, 0, 0)
    anywhere = pl.BlockSpec(memory_space=pltpu.HBM)
    return pl.pallas_call(
        far_body,
        grid=(steps,),
        in_specs=[
            *[pl.BlockSpec(memory_space=pltpu.SMEM)] * 3,
            block,
            block,
            block,
            pl.BlockSpec(memory_space=pltpu.VMEM),
            pl.BlockSpec(memory_space=pltpu.VMEM),
            pl.BlockSpec((width, STEP_COLS), lambda s: (0, steps + s)),
            pl.BlockSpec((width, STEP_COLS), lambda s: (0, 2 * steps + s)),
            pl.BlockSpec((members, width), whole2),
            pl.BlockSpec((fields, width), whole2),
            anywhere,
            anywhere,
        ],
        out_specs=[
            anywhere,
            pl.BlockSpec((members, rows, 128), whole3),
            anywhere,
            pl.BlockSpec((members, padded, rows), whole3),
            pl.BlockSpec((padded, width), whole2),
        ],
        out_shape=[
            jax.ShapeDtypeStruct((members, rows, width), BF16),
            jax.ShapeDtypeStruct((members, rows, 128), F32),
            jax.ShapeDtypeStruct((members, rows, width), BF16),
            jax.ShapeDtypeStruct((members, padded, rows), BF16),
            jax.ShapeDtypeStruct((padded, width), BF16),
        ],
        scratch_shapes=[
            pltpu.VMEM((members * 2 * HALO, width), BF16),
            pltpu.VMEM((2, HALO, HALO), F32),
            pltpu.VMEM((members * 2 * HALO, STEP_COLS), BF16),
            pltpu.VMEM((STEP_COLS // PAIR, members * 2, 2 * HALO, 2 * PAIR), BF16),
            pltpu.VMEM((tall, width), BF16),
            pltpu.VMEM((members, rows, width), BF16),
            pltpu.VMEM((width, width), BF16),
            pltpu.VMEM((members, rows, width), BF16),
            pltpu.VMEM((members, rows, width), BF16),
            pltpu.SemaphoreType.DMA((2,)),
            pltpu.SemaphoreType.DMA((2 * members * rows // HALO,)),
        ],
        compiler_params=pltpu.CompilerParams(vmem_limit_bytes=60 * MIB),
        cost_estimate=pl.CostEstimate(
            flops=15 * 10**9, bytes_accessed=22 * MIB, transcendentals=10**7
        ),
        name="far",
    )(*place, q, o, lse, before, after, w_qkv, w_qkv, noise, dec, latent, w_out)


def crps_body(
    place_ref, count_ref, pred_ref, target_ref, fw_ref, aw_ref, normed_hbm, grad_ref, pieces_ref, normed_ref, padded_ref, sem
):
    fetch = pltpu.make_async_copy(normed_hbm, normed_ref, sem)
    fetch.start()
    bands = count_ref.shape[0]
    first = lax.div(place_ref[0], bands)
    count = count_ref[lax.rem(place_ref[0], bands)]
    ensemble = pred_ref.shape[0] * pred_ref.shape[1]
    own_count = pred_ref.shape[1]
    lead = 1.0 / (ensemble - 1)
    fields, rows = padded_ref.shape
    real = target_ref.shape[0]
    padded_ref[...] = jnp.zeros_like(padded_ref)
    padded_ref[:real] = target_ref[...]
    width = normed_ref.shape[-1]
    target = padded_ref[...]
    used = lax.broadcasted_iota(jnp.int32, (1, rows), 1) < count
    shape = (fields, real)
    diagonal = iota(shape, 0) == iota(shape, 1)
    field_weight = jnp.sum(jnp.where(diagonal, fw_ref[...], 0.0), axis=1, keepdims=True)
    scale = field_weight * jnp.where(used, aw_ref[...], 0.0)

    def slope(gap):
        square = gap * gap + smooth_width * smooth_width
        root = lax.rsqrt(square)
        return gap * root, square * root

    loss = jnp.zeros((fields, rows), F32)
    grads = []
    for own in range(own_count):
        mine = pred_ref[first, own].astype(F32)
        pair_slope = jnp.zeros((fields, rows), F32)
        pair_abs = jnp.zeros((fields, rows), F32)
        for other in range(ensemble):
            s, a = slope(mine - pred_ref[other // own_count, other % own_count].astype(F32))
            pair_slope = pair_slope + s
            pair_abs = pair_abs + a
        s, a = slope(mine - target)
        grad = (scale * (s - pair_slope * lead)).astype(BF16)
        grad_ref[own] = grad
        loss = loss + scale * (a - pair_abs * (0.5 * lead))
        grads.append(grad)
    fetch.wait()
    weight = nn_dot(grads[0], normed_ref[0])
    for own in range(1, own_count):
        weight = weight + nn_dot(grads[own], normed_ref[own])
    tiles = width // 128
    for r in range(0, fields, 8):
        for c in range(tiles):
            piece = weight[r : r + 8, c * 128 : c * 128 + 128]
            pieces_ref[r // 8 * tiles + c] = piece.astype(BF16)
    used_pieces = LOSS_PIECE
    whole = jnp.sum(jnp.sum(loss, axis=0, keepdims=True), axis=1, keepdims=True)
    high = whole.astype(BF16)
    rest = (whole - high.astype(F32)).astype(BF16)
    row = lax.broadcasted_iota(jnp.int32, (8, 128), 0)
    both = jnp.where(row == 0, high.astype(F32), jnp.where(row == 1, rest.astype(F32), 0.0))
    pieces_ref[used_pieces] = both.astype(BF16)
    pieces_ref[used_pieces + 1 :] = jnp.zeros_like(pieces_ref[used_pieces + 1 :])


def crps(place, preds, targets, field_weight, area_weight, normed_out, peers):
    _, own_count, fields, rows = preds.shape
    vmem = pl.BlockSpec(memory_space=pltpu.VMEM)
    return pl.pallas_call(
        crps_body,
        in_specs=[pl.BlockSpec(memory_space=pltpu.SMEM)] * 2
        + [vmem] * 4
        + [pl.BlockSpec(memory_space=pltpu.HBM)],
        out_specs=[vmem] * 2,
        out_shape=[
            jax.ShapeDtypeStruct((own_count, fields, rows), BF16),
            jax.ShapeDtypeStruct((peers, 8, 128), BF16),
        ],
        scratch_shapes=[
            pltpu.VMEM(normed_out.shape, BF16),
            pltpu.VMEM((fields, rows), F32),
            pltpu.SemaphoreType.DMA(()),
        ],
        compiler_params=pltpu.CompilerParams(vmem_limit_bytes=52 * MIB),
        cost_estimate=pl.CostEstimate(
            flops=4 * 10**8, bytes_accessed=4 * MIB, transcendentals=10**6
        ),
        name="crps",
    )(*place[:2], preds, targets, field_weight, area_weight, normed_out)


def backward_body(grad_ref, dec_ref, normalized_ref, inverse_ref, out_ref):
    grad_norm = tn_dot(grad_ref[...], dec_ref[...])
    normalized = normalized_ref[...].astype(F32)
    inverse = inverse_ref[...][:, :1]
    mean = jnp.mean(grad_norm, axis=-1, keepdims=True)
    dotted = jnp.mean(grad_norm * normalized, axis=-1, keepdims=True)
    out_ref[...] = (inverse * (grad_norm - mean - normalized * dotted)).astype(BF16)


def backward(grad, dec, normalized, inverse):
    members, fields, rows = grad.shape
    width = dec.shape[1]
    return pl.pallas_call(
        backward_body,
        grid=(members,),
        in_specs=[
            pl.BlockSpec((None, fields, rows), lambda m: (m, 0, 0)),
            pl.BlockSpec((fields, width), lambda m: (0, 0)),
            pl.BlockSpec((None, rows, width), lambda m: (m, 0, 0)),
            pl.BlockSpec((None, rows, 128), lambda m: (m, 0, 0)),
        ],
        out_specs=pl.BlockSpec((None, rows, width), lambda m: (m, 0, 0)),
        out_shape=jax.ShapeDtypeStruct((members, rows, width), BF16),
        compiler_params=pltpu.CompilerParams(vmem_limit_bytes=32 * MIB),
        cost_estimate=pl.CostEstimate(
            flops=5 * 10**8, bytes_accessed=5 * MIB, transcendentals=0
        ),
        name="backward",
    )(grad, dec, normalized, inverse)


def share_body(rank_ref, parts_ref, spread_ref):
    peers = parts_ref.shape[0]
    mine = jnp.sum(parts_ref[...].astype(F32), axis=0)
    row = iota(mine.shape, 0)
    loss = jnp.sum(jnp.where(row < 2, mine, 0.0), axis=0, keepdims=True)
    rounded = loss.astype(BF16).astype(F32)
    as_loss = jnp.where(row == 0, rounded, jnp.where(row == 1, loss - rounded, 0.0))
    mine = jnp.where(rank_ref[0] == LOSS_PIECE, as_loss, mine).astype(BF16)
    spread_ref[...] = jnp.broadcast_to(mine[None], spread_ref.shape)


def finish_body(pieces_ref, weight_ref, loss_ref, *, tokens):
    fields, width = weight_ref.shape
    tiles = width // 128
    for r in range(0, fields, 8):
        count = min(8, fields - r)
        for c in range(tiles):
            piece = pieces_ref[r // 8 * tiles + c].astype(F32) * (1.0 / tokens)
            weight_ref[r : r + count, c * 128 : c * 128 + 128] = piece[:count]
    loss = jnp.sum(pieces_ref[LOSS_PIECE].astype(F32), axis=0, keepdims=True) * (1.0 / tokens)
    loss_ref[0, 0] = jnp.max(loss)


def summed(place, pieces, fields, width, tokens):
    axes = ("mem", "lat")
    vmem = pl.BlockSpec(memory_space=pltpu.VMEM)
    smem = pl.BlockSpec(memory_space=pltpu.SMEM)
    params = pltpu.CompilerParams(vmem_limit_bytes=16 * MIB)
    parts = lax.all_to_all(pieces, axes, split_axis=0, concat_axis=0, tiled=True)
    spread = pl.pallas_call(
        share_body,
        in_specs=[smem, vmem],
        out_specs=vmem,
        out_shape=jax.ShapeDtypeStruct(pieces.shape, BF16),
        compiler_params=params,
        name="share",
    )(place[0], parts)
    whole = lax.all_to_all(spread, axes, split_axis=0, concat_axis=0, tiled=True)
    return pl.pallas_call(
        functools.partial(finish_body, tokens=tokens),
        in_specs=[vmem],
        out_specs=[vmem, smem],
        out_shape=[
            jax.ShapeDtypeStruct((fields, width), F32),
            jax.ShapeDtypeStruct((1, 1), F32),
        ],
        compiler_params=params,
        name="finish",
    )(whole)


def local(
    latent,
    member_noise,
    w_qkv,
    w_out,
    dec_weight,
    targets,
    area_weight,
    field_weight,
    band_count,
    band_window,
):
    members, rows, width = latent.shape
    bands = lax.axis_size("lat")
    fields = dec_weight.shape[0]
    up = [(i, i + 1) for i in range(bands - 1)]
    down = [(j, i) for i, j in up]
    before = lax.ppermute(latent[:, rows - HALO :], "lat", up)
    after = lax.ppermute(latent[:, :HALO], "lat", down)
    place = (lax.axis_index(("mem", "lat")).reshape(1), band_count, band_window)
    q, o, lse = near(place, latent, w_qkv)
    normalized, inverse, normed_out, predicted, dec = far(
        place, q, o, lse, before, after, w_qkv, member_noise, dec_weight, latent, w_out
    )
    preds = lax.all_gather(predicted, "mem", axis=0)
    peers = lax.axis_size("mem") * bands
    grad, pieces = crps(
        place, preds, targets, field_weight[None, :], area_weight[None, :], normed_out, peers
    )
    weight, loss = summed(place, pieces, fields, width, rows * bands)
    grad_hidden = backward(grad, dec, normalized, inverse)
    return grad_hidden, weight, loss.reshape(())


def solution(mesh):
    return jax.shard_map(
        local,
        mesh=mesh,
        in_specs=(
            P("mem", "lat", None),
            P("mem", None),
            P(),
            P(),
            P(),
            P(None, "lat"),
            P("lat"),
            P(),
            P(),
            P("lat", None),
        ),
        out_specs=(P("mem", "lat", None), P(), P()),
        check_vma=False,
    )
```

profile of v0, /device:TPU:1, one launch (start us, length us, event | category | flops | bytes accessed | tf_op | source)
XLA Modules:
  0.0 110.5 jit_solution(10484507933939699750)
XLA Ops:
  0.6 1.7 %fusion = (bf16[2,256,1024]{2,1,0:T(8,128)(2,1)S(1)}, bf16[2,256,1024]{2,1,0:T(8,128)(2,1)S(1)}) fusion(bf16[2,512,1024]{2,1,0:T(8,128)(2,1)} %latent_hbm.1), kind=kLoop, calls=%fused_computation | loop fusion | bytes 4194304 | tf_op jit(solution)/shard_map/slice | solution.py:568
  2.4 1.3 %collective-permute-start.1 = (bf16[2,256,1024]{2,1,0:T(8,128)(2,1)S(1)}, bf16[2,256,1024]{2,1,0:T(8,128)(2,1)S(1)}, u32[]{:S(2)}, u32[]{:S(2)}) collective-permute-start(bf16[2,256,1024]{2,1,0:T(8,128)(2,1)S(1)} %get-tuple-element.27), channel_id=1, source_target_pairs={{1,0},{2,1},{3,2},{4,3},{5,4},{6,5},{7,6},{8,7},{9,8},{10,9},{11,1... | collective-permute-start | bytes 3145736 | tf_op jit(solution)/shard_map/ppermute | solution.py:568
  3.7 5.6 %collective-permute-start = (bf16[2,256,1024]{2,1,0:T(8,128)(2,1)S(1)}, bf16[2,256,1024]{2,1,0:T(8,128)(2,1)}, u32[]{:S(2)}, u32[]{:S(2)}) collective-permute-start(bf16[2,256,1024]{2,1,0:T(8,128)(2,1)S(1)} %get-tuple-element.28), channel_id=1, source_target_pairs={{0,1},{1,2},{2,3},{3,4},{4,5},{5,6},{6,7},{7,8},{8,9},{9,10},{10,1... | collective-permute-start | bytes 3145736 | tf_op jit(solution)/shard_map/ppermute | solution.py:567
  9.3 23.0 %near.1 = (bf16[1024,1024]{1,0:T(8,128)(2,1)}, bf16[1024,1024]{1,0:T(8,128)(2,1)}, f32[1024,1024]{1,0:T(8,128)}) custom-call(s32[1]{0:T(128)} %bitcast.place_ref.rank_ref, s32[32]{0:T(128)} %count_ref.5, s32[1,2]{1,0:T(1,128)} %window_ref.3, bf16[1024,1024]{1,0:T(8,128)(2,1)} %bitcast.9, bf16[1024,3072]{1,0:T(8,128)(2,1)} %wv_ref.3, ...), custom_call_target="tpu_custom_call" | custom-call | flops 20000000000 | bytes 16777216 | tf_op jit(solution)/shard_map/near/pallas_call | solution.py:161
  32.3 0.0 collective-permute-done.1.after_ref
  32.3 0.0 copy-start.7
  32.3 0.0 collective-permute-done.before_ref
  32.3 1.0 copy-done.7
  33.3 0.0 copy-start.2
  33.3 0.0 copy-start.4
  33.3 0.0 copy-start.5
  33.3 0.0 copy-start.6
  33.3 21.2 %far.1 = (bf16[2,512,1024]{2,1,0:T(8,128)(2,1)}, f32[2,512,128]{2,1,0:T(8,128)}, bf16[2,512,1024]{2,1,0:T(8,128)(2,1)}, bf16[2,104,512]{2,1,0:T(8,128)(2,1)}, bf16[104,1024]{1,0:T(8,128)(2,1)}) custom-call(s32[1]{0:T(128)} %bitcast.place_ref.rank_ref, s32[32]{0:T(128)} %count_ref.5, s32[1,2]{1,0:T(1,128)} %window_ref.3, ...), custom_call_target="tpu_custom_call" | custom-call | flops 15000000512 | bytes 23068672 | tf_op jit(solution)/shard_map/far/pallas_call | solution.py:328
  54.6 10.4 %all-gather = bf16[8,104,512]{2,1,0:T(8,128)(2,1)S(1)} all-gather(bf16[2,104,512]{2,1,0:T(8,128)(2,1)} %get-tuple-element.18), channel_id=2, replica_groups=mesh['mem'=4,'lat'=32] {'mem'}, dimensions={0}, use_global_device_ids=true | all-gather | bytes 1064960 | tf_op jit(solution)/shard_map/all_gather | solution.py:574
  65.0 0.0 copy-done.2
  65.0 0.0 copy-done.4
  65.0 0.0 copy-done.5
  65.0 0.0 copy-done.6
  65.0 0.0 copy-start
  65.0 0.0 copy-start.1
  65.0 0.0 copy-start.3
  65.0 2.9 %crps.1 = (bf16[2,104,512]{2,1,0:T(8,128)(2,1)S(1)}, bf16[128,8,128]{2,1,0:T(8,128)(2,1)S(1)}) custom-call(s32[1]{0:T(128)} %bitcast.place_ref.rank_ref, s32[32]{0:T(128)S(1)} %copy-done.5, bf16[4,2,104,512]{3,2,1,0:T(8,128)(2,1)S(1)} %bitcast.6, f32[100,512]{1,0:T(8,128)S(1)} %copy-done.2, f32[1,100]{1,0:T(1,128)S(1)} %bitcast.8, f32[1,512]{1,0:T(1,128)S(1)} %bitcast.7, ...), custom_call_target="tpu_custom_call" | custom-call | flops 400000000 | bytes 4194304 | tf_op jit(solution)/shard_map/crps/pallas_call | solution.py:445
  67.9 25.6 %all_to_all.10.parts_ref = bf16[128,8,128]{2,1,0:T(8,128)(2,1)S(1)} all-to-all(bf16[128,8,128]{2,1,0:T(8,128)(2,1)S(1)} %get-tuple-element.24), channel_id=1, replica_groups=mesh['mem'=4,'lat'=32] {'mem','lat'}, dimensions={0} | all-to-all | bytes 524288 | tf_op jit(solution)/shard_map/all_to_all | solution.py:527
  93.5 0.9 share.1
  94.4 3.9 %all-to-all-start.1 = ((bf16[128,8,128]{2,1,0:T(8,128)(2,1)}), bf16[128,8,128]{2,1,0:T(8,128)(2,1)S(1)}, u32[]{:S(2)}, u32[]{:S(2)}) async-start(bf16[128,8,128]{2,1,0:T(8,128)(2,1)} %share.1), calls=%async_computation.1 | async-start | bytes 524288 | tf_op jit(solution)/shard_map/all_to_all | solution.py:536
  98.3 0.0 copy-done
  98.3 0.0 copy-done.1
  98.3 0.0 copy-done.3
  98.3 2.8 %backward.1 = bf16[2,512,1024]{2,1,0:T(8,128)(2,1)} custom-call(bf16[2,104,512]{2,1,0:T(8,128)(2,1)S(1)} %get-tuple-element.20.grad_ref, bf16[104,1024]{1,0:T(8,128)(2,1)S(1)} %copy-done.3, bf16[2,512,1024]{2,1,0:T(8,128)(2,1)S(1)} %copy-done, f32[2,512,128]{2,1,0:T(8,128)S(1)} %copy-done.1), custom_call_target="tpu_custom_call" | custom-call | flops 500000000 | bytes 5242880 | tf_op jit(solution)/shard_map/backward/pallas_call | solution.py:480
  101.1 8.4 %all-to-all-done.1.pieces_ref = bf16[128,8,128]{2,1,0:T(8,128)(2,1)S(1)} async-done(((bf16[128,8,128]{2,1,0:T(8,128)(2,1)}), bf16[128,8,128]{2,1,0:T(8,128)(2,1)S(1)}, u32[]{:S(2)}, u32[]{:S(2)}) %all-to-all-start.1) | async-done | bytes 262176 | tf_op jit(solution)/shard_map/all_to_all | solution.py:536
  109.6 0.8 finish.1
Async XLA Ops:
  2.4 29.9 %collective-permute-start.1 = (bf16[2,256,1024]{2,1,0:T(8,128)(2,1)S(1)}, bf16[2,256,1024]{2,1,0:T(8,128)(2,1)S(1)}, u32[]{:S(2)}, u32[]{:S(2)}) collective-permute-start(bf16[2,256,1024]{2,1,0:T(8,128)(2,1)S(1)} %get-tuple-element.27), channel_id=1, source_target_pairs={{1,0},{2,1},{3,2},{4,3},{5,4},{6,5},{7,6},{8,7},{9,8},{10,9},{11,1... | collective-permute-start | bytes 3145736 | tf_op jit(solution)/shard_map/ppermute | solution.py:568
  3.7 28.7 %collective-permute-start = (bf16[2,256,1024]{2,1,0:T(8,128)(2,1)S(1)}, bf16[2,256,1024]{2,1,0:T(8,128)(2,1)}, u32[]{:S(2)}, u32[]{:S(2)}) collective-permute-start(bf16[2,256,1024]{2,1,0:T(8,128)(2,1)S(1)} %get-tuple-element.28), channel_id=1, source_target_pairs={{0,1},{1,2},{2,3},{3,4},{4,5},{5,6},{6,7},{7,8},{8,9},{9,10},{10,1... | collective-permute-start | bytes 3145736 | tf_op jit(solution)/shard_map/ppermute | solution.py:567
  32.3 1.0 copy-start.7
  33.3 31.7 %copy-start.2 = (f32[100,512]{1,0:T(8,128)S(1)}, f32[100,512]{1,0:T(8,128)}, u32[]{:S(2)}) copy-start(f32[100,512]{1,0:T(8,128)} %target_ref.1) | copy-start | bytes 614404
  33.3 31.7 %copy-start.4 = (f32[512]{0:T(512)S(1)}, f32[512]{0:T(512)}, u32[]{:S(2)}) copy-start(f32[512]{0:T(512)} %param.16) | copy-start | bytes 6148
  33.3 31.7 %copy-start.5 = (s32[32]{0:T(128)S(1)}, s32[32]{0:T(128)}, u32[]{:S(2)}) copy-start(s32[32]{0:T(128)} %count_ref.5) | copy-start | bytes 388
  33.3 31.7 %copy-start.6 = (f32[100]{0:T(128)S(1)}, f32[100]{0:T(128)}, u32[]{:S(2)}) copy-start(f32[100]{0:T(128)} %param.17) | copy-start | bytes 1204
  65.0 33.3 %copy-start = (bf16[2,512,1024]{2,1,0:T(8,128)(2,1)S(1)}, bf16[2,512,1024]{2,1,0:T(8,128)(2,1)}, u32[]{:S(2)}) copy-start(bf16[2,512,1024]{2,1,0:T(8,128)(2,1)} %get-tuple-element.22.normalized_ref) | copy-start | bytes 6291460
  65.0 33.3 %copy-start.1 = (f32[2,512,128]{2,1,0:T(8,128)S(1)}, f32[2,512,128]{2,1,0:T(8,128)}, u32[]{:S(2)}) copy-start(f32[2,512,128]{2,1,0:T(8,128)} %get-tuple-element.23.inverse_ref) | copy-start | bytes 1572868
  65.0 33.3 %copy-start.3 = (bf16[104,1024]{1,0:T(8,128)(2,1)S(1)}, bf16[104,1024]{1,0:T(8,128)(2,1)}, u32[]{:S(2)}) copy-start(bf16[104,1024]{1,0:T(8,128)(2,1)} %get-tuple-element.21.dec_ref) | copy-start | bytes 638980
  94.4 15.2 %all-to-all-start.1 = ((bf16[128,8,128]{2,1,0:T(8,128)(2,1)}), bf16[128,8,128]{2,1,0:T(8,128)(2,1)S(1)}, u32[]{:S(2)}, u32[]{:S(2)}) async-start(bf16[128,8,128]{2,1,0:T(8,128)(2,1)} %share.1), calls=%async_computation.1 | async-start | bytes 524288 | tf_op jit(solution)/shard_map/all_to_all | solution.py:536
where the time goes:
time: 111 us
  Pallas kernels  51.6 us (46%)
  blocking collectives  36 us (32%)
  starting transfers between devices  10.8 us (10%)
  waiting for transfers between devices  8.45 us (8%)
  local copies, waits for them, and re-layouts  2.74 us (2%)
    all_to_all x1, blocking collectives, summed(): lax.all_to_all(pieces, axes, split_axis=0, concat_axis=0, tiled=True)  25.6 us
    pallas_call x1, Pallas kernels, near(): pl.pallas_call(near_body, grid=(steps,), in_specs=[*[pl.BlockSpec(memory_...  23 us
    pallas_call x1, Pallas kernels, far(): pl.pallas_call(far_body, grid=(steps,), in_specs=[*[pl.BlockSpec(memory_s...  21.2 us
    all_gather x1, blocking collectives, local(): preds = lax.all_gather(predicted, 'mem', axis=0)  10.4 us
    all_to_all x1, waiting for transfers between devices, summed(): lax.all_to_all(spread, axes, split_axis=0, concat_axis=0, tiled=True)  8.44 us
    ppermute x1, starting transfers between devices, local(): before = lax.ppermute(latent[:, rows - HALO:], 'lat', up)  5.64 us
    all_to_all x1, starting transfers between devices, summed(): lax.all_to_all(spread, axes, split_axis=0, concat_axis=0, tiled=True)  3.91 us
    pallas_call x1, Pallas kernels, crps(): pl.pallas_call(crps_body, in_specs=[pl.BlockSpec(memory_space=pltpu.SMEM)...  2.87 us
  transfers between devices with their start and end apart: 3, of which 1 were waited for; matrix products, arithmetic and copies ran while one was open for 0% of the time, Pallas kernels for 23%

commit v1 on v0

--- a/solution.py
+++ b/solution.py
@@ -195,8 +195,8 @@
     q_ref,
     o_ref,
     lse_ref,
+    after_ref,
     before_ref,
-    after_ref,
     wk_ref,
     wv_ref,
     noise_ref,
@@ -315,7 +315,7 @@
             copy.wait()
 
 
-def far(place, q, o, lse, before, after, w_qkv, noise, dec, latent, w_out):
+def far(place, q, o, lse, after, before, w_qkv, noise, dec, latent, w_out):
     members, rows, width = latent.shape
     tall = members * rows
     fields = dec.shape[0]
@@ -374,7 +374,7 @@
             flops=15 * 10**9, bytes_accessed=22 * MIB, transcendentals=10**7
         ),
         name="far",
-    )(*place, q, o, lse, before, after, w_qkv, w_qkv, noise, dec, latent, w_out)
+    )(*place, q, o, lse, after, before, w_qkv, w_qkv, noise, dec, latent, w_out)
 
 
 def crps_body(
@@ -569,7 +569,7 @@
     place = (lax.axis_index(("mem", "lat")).reshape(1), band_count, band_window)
     q, o, lse = near(place, latent, w_qkv)
     normalized, inverse, normed_out, predicted, dec = far(
-        place, q, o, lse, before, after, w_qkv, member_noise, dec_weight, latent, w_out
+        place, q, o, lse, after, before, w_qkv, member_noise, dec_weight, latent, w_out
     )
     preds = lax.all_gather(predicted, "mem", axis=0)
     peers = lax.axis_size("mem") * bands

time: 111 us -> 109 us (0.982)
  starting transfers between devices: 10.8 us -> 9.3 us
  waiting for transfers between devices: 8.45 us -> 9.8 us
  blocking collectives: 36 us -> 34.8 us
    all_to_all x1, blocking collectives: 25.6 us -> 24 us  [summed(): lax.all_to_all(pieces, axes, split_axis=0, concat_axis=0, tiled=True)]
    ppermute x1, starting transfers between devices: 5.64 us -> 4.1 us  [local(): before = lax.ppermute(latent[:, rows - HALO:], 'lat', up)]
    ppermute x1, waiting for transfers between devices: 0.01 us -> 1.36 us  [local(): after = lax.ppermute(latent[:, :HALO], 'lat', down)]
  transfers between devices with their start and end apart: 3 -> 3, of which waited for: 1 -> 2; matrix products, arithmetic and copies ran while one was open for 0% -> 0% of each run, Pallas kernels for 23% -> 24%
where the time goes in v1:
time: 109 us; the launch traced here: 108 us
  Pallas kernels  51.6 us (47%)
  blocking collectives  34.8 us (32%)
  waiting for transfers between devices  9.8 us (9%)
  starting transfers between devices  9.3 us (9%)
  local copies, waits for them, and re-layouts  1.75 us (2%)
    all_to_all x1, blocking collectives, summed(): lax.all_to_all(pieces, axes, split_axis=0, concat_axis=0, tiled=True)  24 us
    pallas_call x1, Pallas kernels, near(): pl.pallas_call(near_body, grid=(steps,), in_specs=[*[pl.BlockSpec(memory_...  23 us
    pallas_call x1, Pallas kernels, far(): pl.pallas_call(far_body, grid=(steps,), in_specs=[*[pl.BlockSpec(memory_s...  21.2 us
    all_gather x1, blocking collectives, local(): preds = lax.all_gather(predicted, 'mem', axis=0)  10.9 us
    all_to_all x1, waiting for transfers between devices, summed(): lax.all_to_all(spread, axes, split_axis=0, concat_axis=0, tiled=True)  8.44 us
    ppermute x1, starting transfers between devices, local(): before = lax.ppermute(latent[:, rows - HALO:], 'lat', up)  4.1 us
    all_to_all x1, starting transfers between devices, summed(): lax.all_to_all(spread, axes, split_axis=0, concat_axis=0, tiled=True)  3.91 us
    pallas_call x1, Pallas kernels, crps(): pl.pallas_call(crps_body, in_specs=[pl.BlockSpec(memory_space=pltpu.SMEM)...  2.87 us
  transfers between devices with their start and end apart: 3, of which 2 were waited for; matrix products, arithmetic and copies ran while one was open for 0% of the time, Pallas kernels for 24%

profile of v1, /device:TPU:1, one launch (start us, length us, event | category | flops | bytes accessed | tf_op | source)
XLA Modules:
  0.0 108.3 jit_solution(6958384294476660456)
XLA Ops:
  0.6 1.7 %fusion = (bf16[2,256,1024]{2,1,0:T(8,128)(2,1)S(1)}, bf16[2,256,1024]{2,1,0:T(8,128)(2,1)S(1)}) fusion(bf16[2,512,1024]{2,1,0:T(8,128)(2,1)} %latent_hbm.1), kind=kLoop, calls=%fused_computation | loop fusion | bytes 4194304 | tf_op jit(solution)/shard_map/slice | solution.py:567
  2.4 4.1 %collective-permute-start.1 = (bf16[2,256,1024]{2,1,0:T(8,128)(2,1)S(1)}, bf16[2,256,1024]{2,1,0:T(8,128)(2,1)S(1)}, u32[]{:S(2)}, u32[]{:S(2)}) collective-permute-start(bf16[2,256,1024]{2,1,0:T(8,128)(2,1)S(1)} %get-tuple-element.27), channel_id=1, source_target_pairs={{0,1},{1,2},{2,3},{3,4},{4,5},{5,6},{6,7},{7,8},{8,9},{9,10},{10,1... | collective-permute-start | bytes 3145736 | tf_op jit(solution)/shard_map/ppermute | solution.py:567
  6.5 1.3 %collective-permute-start = (bf16[2,256,1024]{2,1,0:T(8,128)(2,1)S(1)}, bf16[2,256,1024]{2,1,0:T(8,128)(2,1)}, u32[]{:S(2)}, u32[]{:S(2)}) collective-permute-start(bf16[2,256,1024]{2,1,0:T(8,128)(2,1)S(1)} %get-tuple-element.28), channel_id=1, source_target_pairs={{1,0},{2,1},{3,2},{4,3},{5,4},{6,5},{7,6},{8,7},{9,8},{10,9},{11,1... | collective-permute-start | bytes 3145736 | tf_op jit(solution)/shard_map/ppermute | solution.py:568
  7.8 23.0 %near.1 = (bf16[1024,1024]{1,0:T(8,128)(2,1)}, bf16[1024,1024]{1,0:T(8,128)(2,1)}, f32[1024,1024]{1,0:T(8,128)}) custom-call(s32[1]{0:T(128)} %bitcast.place_ref.rank_ref, s32[32]{0:T(128)} %count_ref.5, s32[1,2]{1,0:T(1,128)} %window_ref.3, bf16[1024,1024]{1,0:T(8,128)(2,1)} %bitcast.9, bf16[1024,3072]{1,0:T(8,128)(2,1)} %wv_ref.3, ...), custom_call_target="tpu_custom_call" | custom-call | flops 20000000000 | bytes 16777216 | tf_op jit(solution)/shard_map/near/pallas_call | solution.py:161
  30.8 0.0 collective-permute-done.1.before_ref
  30.8 0.0 copy-start.7
  30.8 1.4 %collective-permute-done.after_ref = bf16[2,256,1024]{2,1,0:T(8,128)(2,1)} collective-permute-done((bf16[2,256,1024]{2,1,0:T(8,128)(2,1)S(1)}, bf16[2,256,1024]{2,1,0:T(8,128)(2,1)}, u32[]{:S(2)}, u32[]{:S(2)}) %collective-permute-start) | collective-permute-done | bytes 1048608 | tf_op jit(solution)/shard_map/ppermute | solution.py:568
  32.2 0.0 copy-done.7
  32.2 0.0 copy-start.2
  32.2 0.0 copy-start.4
  32.2 0.0 copy-start.5
  32.2 0.0 copy-start.6
  32.2 21.2 %far.1 = (bf16[2,512,1024]{2,1,0:T(8,128)(2,1)}, f32[2,512,128]{2,1,0:T(8,128)}, bf16[2,512,1024]{2,1,0:T(8,128)(2,1)}, bf16[2,104,512]{2,1,0:T(8,128)(2,1)}, bf16[104,1024]{1,0:T(8,128)(2,1)}) custom-call(s32[1]{0:T(128)} %bitcast.place_ref.rank_ref, s32[32]{0:T(128)} %count_ref.5, s32[1,2]{1,0:T(1,128)} %window_ref.3, ...), custom_call_target="tpu_custom_call" | custom-call | flops 15000000512 | bytes 23068672 | tf_op jit(solution)/shard_map/far/pallas_call | solution.py:328
  53.4 10.9 %all-gather = bf16[8,104,512]{2,1,0:T(8,128)(2,1)S(1)} all-gather(bf16[2,104,512]{2,1,0:T(8,128)(2,1)} %get-tuple-element.18), channel_id=2, replica_groups=mesh['mem'=4,'lat'=32] {'mem'}, dimensions={0}, use_global_device_ids=true | all-gather | bytes 1064960 | tf_op jit(solution)/shard_map/all_gather | solution.py:574
  64.3 0.0 copy-done.2
  64.3 0.0 copy-done.4
  64.3 0.0 copy-done.5
  64.3 0.0 copy-done.6
  64.3 0.0 copy-start
  64.3 0.0 copy-start.1
  64.4 0.0 copy-start.3
  64.4 2.9 %crps.1 = (bf16[2,104,512]{2,1,0:T(8,128)(2,1)S(1)}, bf16[128,8,128]{2,1,0:T(8,128)(2,1)S(1)}) custom-call(s32[1]{0:T(128)} %bitcast.place_ref.rank_ref, s32[32]{0:T(128)S(1)} %copy-done.5, bf16[4,2,104,512]{3,2,1,0:T(8,128)(2,1)S(1)} %bitcast.6, f32[100,512]{1,0:T(8,128)S(1)} %copy-done.2, f32[1,100]{1,0:T(1,128)S(1)} %bitcast.8, f32[1,512]{1,0:T(1,128)S(1)} %bitcast.7, ...), custom_call_target="tpu_custom_call" | custom-call | flops 400000000 | bytes 4194304 | tf_op jit(solution)/shard_map/crps/pallas_call | solution.py:445
  67.3 24.0 %all_to_all.10.parts_ref = bf16[128,8,128]{2,1,0:T(8,128)(2,1)S(1)} all-to-all(bf16[128,8,128]{2,1,0:T(8,128)(2,1)S(1)} %get-tuple-element.24), channel_id=1, replica_groups=mesh['mem'=4,'lat'=32] {'mem','lat'}, dimensions={0} | all-to-all | bytes 524288 | tf_op jit(solution)/shard_map/all_to_all | solution.py:527
  91.2 0.9 share.1
  92.1 3.9 %all-to-all-start.1 = ((bf16[128,8,128]{2,1,0:T(8,128)(2,1)}), bf16[128,8,128]{2,1,0:T(8,128)(2,1)S(1)}, u32[]{:S(2)}, u32[]{:S(2)}) async-start(bf16[128,8,128]{2,1,0:T(8,128)(2,1)} %share.1), calls=%async_computation.1 | async-start | bytes 524288 | tf_op jit(solution)/shard_map/all_to_all | solution.py:536
  96.0 0.0 copy-done
  96.0 0.0 copy-done.1
  96.0 0.0 copy-done.3
  96.0 2.8 %backward.1 = bf16[2,512,1024]{2,1,0:T(8,128)(2,1)} custom-call(bf16[2,104,512]{2,1,0:T(8,128)(2,1)S(1)} %get-tuple-element.20.grad_ref, bf16[104,1024]{1,0:T(8,128)(2,1)S(1)} %copy-done.3, bf16[2,512,1024]{2,1,0:T(8,128)(2,1)S(1)} %copy-done, f32[2,512,128]{2,1,0:T(8,128)S(1)} %copy-done.1), custom_call_target="tpu_custom_call" | custom-call | flops 500000000 | bytes 5242880 | tf_op jit(solution)/shard_map/backward/pallas_call | solution.py:480
  98.9 8.4 %all-to-all-done.1.pieces_ref = bf16[128,8,128]{2,1,0:T(8,128)(2,1)S(1)} async-done(((bf16[128,8,128]{2,1,0:T(8,128)(2,1)}), bf16[128,8,128]{2,1,0:T(8,128)(2,1)S(1)}, u32[]{:S(2)}, u32[]{:S(2)}) %all-to-all-start.1) | async-done | bytes 262176 | tf_op jit(solution)/shard_map/all_to_all | solution.py:536
  107.3 0.8 finish.1
Async XLA Ops:
  2.4 28.4 %collective-permute-start.1 = (bf16[2,256,1024]{2,1,0:T(8,128)(2,1)S(1)}, bf16[2,256,1024]{2,1,0:T(8,128)(2,1)S(1)}, u32[]{:S(2)}, u32[]{:S(2)}) collective-permute-start(bf16[2,256,1024]{2,1,0:T(8,128)(2,1)S(1)} %get-tuple-element.27), channel_id=1, source_target_pairs={{0,1},{1,2},{2,3},{3,4},{4,5},{5,6},{6,7},{7,8},{8,9},{9,10},{10,1... | collective-permute-start | bytes 3145736 | tf_op jit(solution)/shard_map/ppermute | solution.py:567
  6.5 25.7 %collective-permute-start = (bf16[2,256,1024]{2,1,0:T(8,128)(2,1)S(1)}, bf16[2,256,1024]{2,1,0:T(8,128)(2,1)}, u32[]{:S(2)}, u32[]{:S(2)}) collective-permute-start(bf16[2,256,1024]{2,1,0:T(8,128)(2,1)S(1)} %get-tuple-element.28), channel_id=1, source_target_pairs={{1,0},{2,1},{3,2},{4,3},{5,4},{6,5},{7,6},{8,7},{9,8},{10,9},{11,1... | collective-permute-start | bytes 3145736 | tf_op jit(solution)/shard_map/ppermute | solution.py:568
  30.8 1.4 %copy-start.7 = (bf16[2,256,1024]{2,1,0:T(8,128)(2,1)}, bf16[2,256,1024]{2,1,0:T(8,128)(2,1)S(1)}, u32[]{:S(2)}) copy-start(bf16[2,256,1024]{2,1,0:T(8,128)(2,1)S(1)} %collective-permute-done.1.before_ref) | copy-start | bytes 3145732
  32.2 32.2 %copy-start.2 = (f32[100,512]{1,0:T(8,128)S(1)}, f32[100,512]{1,0:T(8,128)}, u32[]{:S(2)}) copy-start(f32[100,512]{1,0:T(8,128)} %target_ref.1) | copy-start | bytes 614404
  32.2 32.2 %copy-start.4 = (f32[512]{0:T(512)S(1)}, f32[512]{0:T(512)}, u32[]{:S(2)}) copy-start(f32[512]{0:T(512)} %param.16) | copy-start | bytes 6148
  32.2 32.2 %copy-start.5 = (s32[32]{0:T(128)S(1)}, s32[32]{0:T(128)}, u32[]{:S(2)}) copy-start(s32[32]{0:T(128)} %count_ref.5) | copy-start | bytes 388
  32.2 32.2 %copy-start.6 = (f32[100]{0:T(128)S(1)}, f32[100]{0:T(128)}, u32[]{:S(2)}) copy-start(f32[100]{0:T(128)} %param.17) | copy-start | bytes 1204
  64.3 31.7 %copy-start = (bf16[2,512,1024]{2,1,0:T(8,128)(2,1)S(1)}, bf16[2,512,1024]{2,1,0:T(8,128)(2,1)}, u32[]{:S(2)}) copy-start(bf16[2,512,1024]{2,1,0:T(8,128)(2,1)} %get-tuple-element.22.normalized_ref) | copy-start | bytes 6291460
  64.3 31.7 %copy-start.1 = (f32[2,512,128]{2,1,0:T(8,128)S(1)}, f32[2,512,128]{2,1,0:T(8,128)}, u32[]{:S(2)}) copy-start(f32[2,512,128]{2,1,0:T(8,128)} %get-tuple-element.23.inverse_ref) | copy-start | bytes 1572868
  64.4 31.7 %copy-start.3 = (bf16[104,1024]{1,0:T(8,128)(2,1)S(1)}, bf16[104,1024]{1,0:T(8,128)(2,1)}, u32[]{:S(2)}) copy-start(bf16[104,1024]{1,0:T(8,128)(2,1)} %get-tuple-element.21.dec_ref) | copy-start | bytes 638980
  92.1 15.2 %all-to-all-start.1 = ((bf16[128,8,128]{2,1,0:T(8,128)(2,1)}), bf16[128,8,128]{2,1,0:T(8,128)(2,1)S(1)}, u32[]{:S(2)}, u32[]{:S(2)}) async-start(bf16[128,8,128]{2,1,0:T(8,128)(2,1)} %share.1), calls=%async_computation.1 | async-start | bytes 524288 | tf_op jit(solution)/shard_map/all_to_all | solution.py:536

commit v2 on v1

--- a/solution.py
+++ b/solution.py
@@ -369,7 +369,7 @@
             pltpu.SemaphoreType.DMA((2,)),
             pltpu.SemaphoreType.DMA((2 * members * rows // HALO,)),
         ],
-        compiler_params=pltpu.CompilerParams(vmem_limit_bytes=60 * MIB),
+        compiler_params=pltpu.CompilerParams(vmem_limit_bytes=51 * MIB),
         cost_estimate=pl.CostEstimate(
             flops=15 * 10**9, bytes_accessed=22 * MIB, transcendentals=10**7
         ),

time: 109 us -> 107 us (0.982)
  Pallas kernels: 51.6 us -> 50.2 us
  blocking collectives: 34.8 us -> 33.7 us
    pallas_call x1, Pallas kernels: 21.2 us -> 19.9 us  [far(): pl.pallas_call(far_body, grid=(steps,), in_specs=[*[pl.BlockSpec(memory_s...]
where the time goes in v2:
time: 107 us; the launch traced here: 106 us
  Pallas kernels  50.2 us (47%)
  blocking collectives  33.7 us (31%)
  starting transfers between devices  10.2 us (10%)
  waiting for transfers between devices  9.62 us (9%)
  local copies, waits for them, and re-layouts  1.77 us (2%)
    pallas_call x1, Pallas kernels, near(): pl.pallas_call(near_body, grid=(steps,), in_specs=[*[pl.BlockSpec(memory_...  23.1 us
    all_to_all x1, blocking collectives, summed(): lax.all_to_all(pieces, axes, split_axis=0, concat_axis=0, tiled=True)  23.1 us
    pallas_call x1, Pallas kernels, far(): pl.pallas_call(far_body, grid=(steps,), in_specs=[*[pl.BlockSpec(memory_s...  19.9 us
    all_gather x1, blocking collectives, local(): preds = lax.all_gather(predicted, 'mem', axis=0)  10.7 us
    all_to_all x1, waiting for transfers between devices, summed(): lax.all_to_all(spread, axes, split_axis=0, concat_axis=0, tiled=True)  8.46 us
    ppermute x1, starting transfers between devices, local(): before = lax.ppermute(latent[:, rows - HALO:], 'lat', up)  5.01 us
    all_to_all x1, starting transfers between devices, summed(): lax.all_to_all(spread, axes, split_axis=0, concat_axis=0, tiled=True)  3.91 us
    pallas_call x1, Pallas kernels, backward(): pl.pallas_call(backward_body, grid=(members,), in_specs=[pl.BlockSpec((No...  2.83 us
  transfers between devices with their start and end apart: 3, of which 2 were waited for; matrix products, arithmetic and copies ran while one was open for 0% of the time, Pallas kernels for 24%

profile of v2, /device:TPU:1, one launch (start us, length us, event | category | flops | bytes accessed | tf_op | source)
XLA Modules:
  0.0 106.4 jit_solution(9616355441237926918)
XLA Ops:
  0.6 1.7 %fusion = (bf16[2,256,1024]{2,1,0:T(8,128)(2,1)S(1)}, bf16[2,256,1024]{2,1,0:T(8,128)(2,1)S(1)}) fusion(bf16[2,512,1024]{2,1,0:T(8,128)(2,1)} %latent_hbm.1), kind=kLoop, calls=%fused_computation | loop fusion | bytes 4194304 | tf_op jit(solution)/shard_map/slice | solution.py:567
  2.4 5.0 %collective-permute-start.1 = (bf16[2,256,1024]{2,1,0:T(8,128)(2,1)S(1)}, bf16[2,256,1024]{2,1,0:T(8,128)(2,1)}, u32[]{:S(2)}, u32[]{:S(2)}) collective-permute-start(bf16[2,256,1024]{2,1,0:T(8,128)(2,1)S(1)} %get-tuple-element.27), channel_id=1, source_target_pairs={{0,1},{1,2},{2,3},{3,4},{4,5},{5,6},{6,7},{7,8},{8,9},{9,10},{10,1... | collective-permute-start | bytes 3145736 | tf_op jit(solution)/shard_map/ppermute | solution.py:567
  7.4 1.3 %collective-permute-start = (bf16[2,256,1024]{2,1,0:T(8,128)(2,1)S(1)}, bf16[2,256,1024]{2,1,0:T(8,128)(2,1)S(1)}, u32[]{:S(2)}, u32[]{:S(2)}) collective-permute-start(bf16[2,256,1024]{2,1,0:T(8,128)(2,1)S(1)} %get-tuple-element.28), channel_id=1, source_target_pairs={{1,0},{2,1},{3,2},{4,3},{5,4},{6,5},{7,6},{8,7},{9,8},{10,9},{11,1... | collective-permute-start | bytes 3145736 | tf_op jit(solution)/shard_map/ppermute | solution.py:568
  8.7 0.0 copy-start.3
  8.7 0.0 copy-start.5
  8.7 0.0 copy-start.6
  8.7 0.0 copy-start.7
  8.7 23.1 %near.1 = (bf16[1024,1024]{1,0:T(8,128)(2,1)}, bf16[1024,1024]{1,0:T(8,128)(2,1)}, f32[1024,1024]{1,0:T(8,128)}) custom-call(s32[1]{0:T(128)} %bitcast.place_ref.rank_ref, s32[32]{0:T(128)} %count_ref.5, s32[1,2]{1,0:T(1,128)} %window_ref.3, bf16[1024,1024]{1,0:T(8,128)(2,1)} %bitcast.9, bf16[1024,3072]{1,0:T(8,128)(2,1)} %wv_ref.3, ...), custom_call_target="tpu_custom_call" | custom-call | flops 20000000000 | bytes 16777216 | tf_op jit(solution)/shard_map/near/pallas_call | solution.py:161
  31.8 0.0 collective-permute-done.1.before_ref
  31.8 1.2 %collective-permute-done.after_ref = bf16[2,256,1024]{2,1,0:T(8,128)(2,1)S(1)} collective-permute-done((bf16[2,256,1024]{2,1,0:T(8,128)(2,1)S(1)}, bf16[2,256,1024]{2,1,0:T(8,128)(2,1)S(1)}, u32[]{:S(2)}, u32[]{:S(2)}) %collective-permute-start) | collective-permute-done | bytes 1048608 | tf_op jit(solution)/shard_map/ppermute | solution.py:568
  33.0 0.0 copy-done.3
  33.0 0.0 copy-done.5
  33.0 0.0 copy-done.6
  33.0 0.0 copy-done.7
  33.0 0.0 copy-start.1
  33.0 0.0 copy-start.2
  33.0 0.0 copy-start.4
  33.0 19.9 %far.1 = (bf16[2,512,1024]{2,1,0:T(8,128)(2,1)}, f32[2,512,128]{2,1,0:T(8,128)S(1)}, bf16[2,512,1024]{2,1,0:T(8,128)(2,1)}, bf16[2,104,512]{2,1,0:T(8,128)(2,1)S(1)}, bf16[104,1024]{1,0:T(8,128)(2,1)S(1)}) custom-call(s32[1]{0:T(128)} %bitcast.place_ref.rank_ref, s32[32]{0:T(128)S(1)} %copy-done.3, s32[1,2]{1,0:T(1,128)S(1)} %copy-done.7, ...), custom_call_target="tpu_custom_call" | custom-call | flops 15000000512 | bytes 23068672 | tf_op jit(solution)/shard_map/far/pallas_call | solution.py:328
  52.9 10.7 %all-gather = bf16[8,104,512]{2,1,0:T(8,128)(2,1)S(1)} all-gather(bf16[2,104,512]{2,1,0:T(8,128)(2,1)S(1)} %get-tuple-element.18), channel_id=2, replica_groups=mesh['mem'=4,'lat'=32] {'mem'}, dimensions={0}, use_global_device_ids=true | all-gather | bytes 1064960 | tf_op jit(solution)/shard_map/all_gather | solution.py:574
  63.6 0.0 copy-done.1
  63.6 0.0 copy-done.2
  63.6 0.0 copy-done.4
  63.6 0.0 copy-start
  63.6 2.7 %crps.1 = (bf16[2,104,512]{2,1,0:T(8,128)(2,1)S(1)}, bf16[128,8,128]{2,1,0:T(8,128)(2,1)S(1)}) custom-call(s32[1]{0:T(128)} %bitcast.place_ref.rank_ref, s32[32]{0:T(128)S(1)} %copy-done.3, bf16[4,2,104,512]{3,2,1,0:T(8,128)(2,1)S(1)} %bitcast.6, f32[100,512]{1,0:T(8,128)S(1)} %copy-done.1, f32[1,100]{1,0:T(1,128)S(1)} %bitcast.8, f32[1,512]{1,0:T(1,128)S(1)} %bitcast.7, ...), custom_call_target="tpu_custom_call" | custom-call | flops 400000000 | bytes 4194304 | tf_op jit(solution)/shard_map/crps/pallas_call | solution.py:445
  66.3 23.1 %all_to_all.10.parts_ref = bf16[128,8,128]{2,1,0:T(8,128)(2,1)S(1)} all-to-all(bf16[128,8,128]{2,1,0:T(8,128)(2,1)S(1)} %get-tuple-element.24), channel_id=1, replica_groups=mesh['mem'=4,'lat'=32] {'mem','lat'}, dimensions={0} | all-to-all | bytes 524288 | tf_op jit(solution)/shard_map/all_to_all | solution.py:527
  89.4 0.9 share.1
  90.2 3.9 %all-to-all-start.1 = ((bf16[128,8,128]{2,1,0:T(8,128)(2,1)}), bf16[128,8,128]{2,1,0:T(8,128)(2,1)S(1)}, u32[]{:S(2)}, u32[]{:S(2)}) async-start(bf16[128,8,128]{2,1,0:T(8,128)(2,1)} %share.1), calls=%async_computation.1 | async-start | bytes 524288 | tf_op jit(solution)/shard_map/all_to_all | solution.py:536
  94.2 0.0 copy-done
  94.2 2.8 %backward.1 = bf16[2,512,1024]{2,1,0:T(8,128)(2,1)} custom-call(bf16[2,104,512]{2,1,0:T(8,128)(2,1)S(1)} %get-tuple-element.20.grad_ref, bf16[104,1024]{1,0:T(8,128)(2,1)S(1)} %get-tuple-element.21.dec_ref, bf16[2,512,1024]{2,1,0:T(8,128)(2,1)S(1)} %copy-done, f32[2,512,128]{2,1,0:T(8,128)S(1)} %get-tuple-element.23.inverse_ref), custom_call_target="tpu_custom_call" | custom-call | flops 500000000 | bytes 5242880 | tf_op jit(solution)/shard_map/backward/pallas_call | solution.py:480
  97.0 8.5 %all-to-all-done.1.pieces_ref = bf16[128,8,128]{2,1,0:T(8,128)(2,1)S(1)} async-done(((bf16[128,8,128]{2,1,0:T(8,128)(2,1)}), bf16[128,8,128]{2,1,0:T(8,128)(2,1)S(1)}, u32[]{:S(2)}, u32[]{:S(2)}) %all-to-all-start.1) | async-done | bytes 262176 | tf_op jit(solution)/shard_map/all_to_all | solution.py:536
  105.5 0.8 finish.1
Async XLA Ops:
  2.4 29.4 %collective-permute-start.1 = (bf16[2,256,1024]{2,1,0:T(8,128)(2,1)S(1)}, bf16[2,256,1024]{2,1,0:T(8,128)(2,1)}, u32[]{:S(2)}, u32[]{:S(2)}) collective-permute-start(bf16[2,256,1024]{2,1,0:T(8,128)(2,1)S(1)} %get-tuple-element.27), channel_id=1, source_target_pairs={{0,1},{1,2},{2,3},{3,4},{4,5},{5,6},{6,7},{7,8},{8,9},{9,10},{10,1... | collective-permute-start | bytes 3145736 | tf_op jit(solution)/shard_map/ppermute | solution.py:567
  7.4 25.6 %collective-permute-start = (bf16[2,256,1024]{2,1,0:T(8,128)(2,1)S(1)}, bf16[2,256,1024]{2,1,0:T(8,128)(2,1)S(1)}, u32[]{:S(2)}, u32[]{:S(2)}) collective-permute-start(bf16[2,256,1024]{2,1,0:T(8,128)(2,1)S(1)} %get-tuple-element.28), channel_id=1, source_target_pairs={{1,0},{2,1},{3,2},{4,3},{5,4},{6,5},{7,6},{8,7},{9,8},{10,9},{11,1... | collective-permute-start | bytes 3145736 | tf_op jit(solution)/shard_map/ppermute | solution.py:568
  8.7 24.3 %copy-start.3 = (s32[32]{0:T(128)S(1)}, s32[32]{0:T(128)}, u32[]{:S(2)}) copy-start(s32[32]{0:T(128)} %count_ref.5) | copy-start | bytes 388
  8.7 24.3 %copy-start.5 = (bf16[100,1024]{1,0:T(8,128)(2,1)S(1)}, bf16[100,1024]{1,0:T(8,128)(2,1)}, u32[]{:S(2)}) copy-start(bf16[100,1024]{1,0:T(8,128)(2,1)} %dec_ref.1) | copy-start | bytes 614404
  8.7 24.3 %copy-start.6 = (bf16[2,1024]{1,0:T(2,128)(2,1)S(1)}, bf16[2,1024]{1,0:T(2,128)(2,1)}, u32[]{:S(2)}) copy-start(bf16[2,1024]{1,0:T(2,128)(2,1)} %noise_ref.1) | copy-start | bytes 12292
  8.7 24.3 %copy-start.7 = (s32[1,2]{1,0:T(1,128)S(1)}, s32[1,2]{1,0:T(1,128)}, u32[]{:S(2)}) copy-start(s32[1,2]{1,0:T(1,128)} %window_ref.3) | copy-start | bytes 28
  33.0 30.6 %copy-start.1 = (f32[100,512]{1,0:T(8,128)S(1)}, f32[100,512]{1,0:T(8,128)}, u32[]{:S(2)}) copy-start(f32[100,512]{1,0:T(8,128)} %target_ref.1) | copy-start | bytes 614404
  33.0 30.6 %copy-start.2 = (f32[512]{0:T(512)S(1)}, f32[512]{0:T(512)}, u32[]{:S(2)}) copy-start(f32[512]{0:T(512)} %param.16) | copy-start | bytes 6148
  33.0 30.6 %copy-start.4 = (f32[100]{0:T(128)S(1)}, f32[100]{0:T(128)}, u32[]{:S(2)}) copy-start(f32[100]{0:T(128)} %param.17) | copy-start | bytes 1204
  63.6 30.5 %copy-start = (bf16[2,512,1024]{2,1,0:T(8,128)(2,1)S(1)}, bf16[2,512,1024]{2,1,0:T(8,128)(2,1)}, u32[]{:S(2)}) copy-start(bf16[2,512,1024]{2,1,0:T(8,128)(2,1)} %get-tuple-element.22.normalized_ref) | copy-start | bytes 6291460
  90.2 15.2 %all-to-all-start.1 = ((bf16[128,8,128]{2,1,0:T(8,128)(2,1)}), bf16[128,8,128]{2,1,0:T(8,128)(2,1)S(1)}, u32[]{:S(2)}, u32[]{:S(2)}) async-start(bf16[128,8,128]{2,1,0:T(8,128)(2,1)} %share.1), calls=%async_computation.1 | async-start | bytes 524288 | tf_op jit(solution)/shard_map/all_to_all | solution.py:536

commit v3 on v2

--- a/solution.py
+++ b/solution.py
@@ -180,7 +180,7 @@
             pltpu.VMEM((tall, STEP_COLS), BF16),
             pltpu.VMEM((STEP_COLS // PAIR, members, 2 * rows, 2 * PAIR), BF16),
         ],
-        compiler_params=pltpu.CompilerParams(vmem_limit_bytes=60 * MIB),
+        compiler_params=pltpu.CompilerParams(vmem_limit_bytes=57 * MIB),
         cost_estimate=pl.CostEstimate(
             flops=20 * 10**9, bytes_accessed=16 * MIB, transcendentals=10**7
         ),

time: 107 us -> 107 us (level)
  no operation moved by 1% of the time
where the time goes in v3:
time: 107 us; the launch traced here: 106 us
  Pallas kernels  50.2 us (47%)
  blocking collectives  33.7 us (31%)
  starting transfers between devices  10.2 us (10%)
  waiting for transfers between devices  9.62 us (9%)
  local copies, waits for them, and re-layouts  1.77 us (2%)
    pallas_call x1, Pallas kernels, near(): pl.pallas_call(near_body, grid=(steps,), in_specs=[*[pl.BlockSpec(memory_...  23.1 us
    all_to_all x1, blocking collectives, summed(): lax.all_to_all(pieces, axes, split_axis=0, concat_axis=0, tiled=True)  23.1 us
    pallas_call x1, Pallas kernels, far(): pl.pallas_call(far_body, grid=(steps,), in_specs=[*[pl.BlockSpec(memory_s...  19.9 us
    all_gather x1, blocking collectives, local(): preds = lax.all_gather(predicted, 'mem', axis=0)  10.7 us
    all_to_all x1, waiting for transfers between devices, summed(): lax.all_to_all(spread, axes, split_axis=0, concat_axis=0, tiled=True)  8.46 us
    ppermute x1, starting transfers between devices, local(): before = lax.ppermute(latent[:, rows - HALO:], 'lat', up)  5.01 us
    all_to_all x1, starting transfers between devices, summed(): lax.all_to_all(spread, axes, split_axis=0, concat_axis=0, tiled=True)  3.91 us
    pallas_call x1, Pallas kernels, backward(): pl.pallas_call(backward_body, grid=(members,), in_specs=[pl.BlockSpec((No...  2.83 us
  transfers between devices with their start and end apart: 3, of which 2 were waited for; matrix products, arithmetic and copies ran while one was open for 0% of the time, Pallas kernels for 24%

profile of v3, /device:TPU:1, one launch (start us, length us, event | category | flops | bytes accessed | tf_op | source)
XLA Modules:
  0.0 106.4 jit_solution(11081068244296945278)
XLA Ops:
  0.6 1.7 %fusion = (bf16[2,256,1024]{2,1,0:T(8,128)(2,1)S(1)}, bf16[2,256,1024]{2,1,0:T(8,128)(2,1)S(1)}) fusion(bf16[2,512,1024]{2,1,0:T(8,128)(2,1)} %latent_hbm.1), kind=kLoop, calls=%fused_computation | loop fusion | bytes 4194304 | tf_op jit(solution)/shard_map/slice | solution.py:567
  2.4 5.0 %collective-permute-start.1 = (bf16[2,256,1024]{2,1,0:T(8,128)(2,1)S(1)}, bf16[2,256,1024]{2,1,0:T(8,128)(2,1)}, u32[]{:S(2)}, u32[]{:S(2)}) collective-permute-start(bf16[2,256,1024]{2,1,0:T(8,128)(2,1)S(1)} %get-tuple-element.27), channel_id=1, source_target_pairs={{0,1},{1,2},{2,3},{3,4},{4,5},{5,6},{6,7},{7,8},{8,9},{9,10},{10,1... | collective-permute-start | bytes 3145736 | tf_op jit(solution)/shard_map/ppermute | solution.py:567
  7.4 1.3 %collective-permute-start = (bf16[2,256,1024]{2,1,0:T(8,128)(2,1)S(1)}, bf16[2,256,1024]{2,1,0:T(8,128)(2,1)S(1)}, u32[]{:S(2)}, u32[]{:S(2)}) collective-permute-start(bf16[2,256,1024]{2,1,0:T(8,128)(2,1)S(1)} %get-tuple-element.28), channel_id=1, source_target_pairs={{1,0},{2,1},{3,2},{4,3},{5,4},{6,5},{7,6},{8,7},{9,8},{10,9},{11,1... | collective-permute-start | bytes 3145736 | tf_op jit(solution)/shard_map/ppermute | solution.py:568
  8.7 0.0 copy-start.3
  8.7 0.0 copy-start.5
  8.7 0.0 copy-start.6
  8.7 0.0 copy-start.7
  8.7 23.1 %near.1 = (bf16[1024,1024]{1,0:T(8,128)(2,1)}, bf16[1024,1024]{1,0:T(8,128)(2,1)}, f32[1024,1024]{1,0:T(8,128)}) custom-call(s32[1]{0:T(128)} %bitcast.place_ref.rank_ref, s32[32]{0:T(128)} %count_ref.5, s32[1,2]{1,0:T(1,128)} %window_ref.3, bf16[1024,1024]{1,0:T(8,128)(2,1)} %bitcast.9, bf16[1024,3072]{1,0:T(8,128)(2,1)} %wv_ref.3, ...), custom_call_target="tpu_custom_call" | custom-call | flops 20000000000 | bytes 16777216 | tf_op jit(solution)/shard_map/near/pallas_call | solution.py:161
  31.8 0.0 collective-permute-done.1.before_ref
  31.8 1.2 %collective-permute-done.after_ref = bf16[2,256,1024]{2,1,0:T(8,128)(2,1)S(1)} collective-permute-done((bf16[2,256,1024]{2,1,0:T(8,128)(2,1)S(1)}, bf16[2,256,1024]{2,1,0:T(8,128)(2,1)S(1)}, u32[]{:S(2)}, u32[]{:S(2)}) %collective-permute-start) | collective-permute-done | bytes 1048608 | tf_op jit(solution)/shard_map/ppermute | solution.py:568
  33.0 0.0 copy-done.3
  33.0 0.0 copy-done.5
  33.0 0.0 copy-done.6
  33.0 0.0 copy-done.7
  33.0 0.0 copy-start.1
  33.0 0.0 copy-start.2
  33.0 0.0 copy-start.4
  33.0 19.9 %far.1 = (bf16[2,512,1024]{2,1,0:T(8,128)(2,1)}, f32[2,512,128]{2,1,0:T(8,128)S(1)}, bf16[2,512,1024]{2,1,0:T(8,128)(2,1)}, bf16[2,104,512]{2,1,0:T(8,128)(2,1)S(1)}, bf16[104,1024]{1,0:T(8,128)(2,1)S(1)}) custom-call(s32[1]{0:T(128)} %bitcast.place_ref.rank_ref, s32[32]{0:T(128)S(1)} %copy-done.3, s32[1,2]{1,0:T(1,128)S(1)} %copy-done.7, ...), custom_call_target="tpu_custom_call" | custom-call | flops 15000000512 | bytes 23068672 | tf_op jit(solution)/shard_map/far/pallas_call | solution.py:328
  52.9 10.7 %all-gather = bf16[8,104,512]{2,1,0:T(8,128)(2,1)S(1)} all-gather(bf16[2,104,512]{2,1,0:T(8,128)(2,1)S(1)} %get-tuple-element.18), channel_id=2, replica_groups=mesh['mem'=4,'lat'=32] {'mem'}, dimensions={0}, use_global_device_ids=true | all-gather | bytes 1064960 | tf_op jit(solution)/shard_map/all_gather | solution.py:574
  63.6 0.0 copy-done.1
  63.6 0.0 copy-done.2
  63.6 0.0 copy-done.4
  63.6 0.0 copy-start
  63.6 2.7 %crps.1 = (bf16[2,104,512]{2,1,0:T(8,128)(2,1)S(1)}, bf16[128,8,128]{2,1,0:T(8,128)(2,1)S(1)}) custom-call(s32[1]{0:T(128)} %bitcast.place_ref.rank_ref, s32[32]{0:T(128)S(1)} %copy-done.3, bf16[4,2,104,512]{3,2,1,0:T(8,128)(2,1)S(1)} %bitcast.6, f32[100,512]{1,0:T(8,128)S(1)} %copy-done.1, f32[1,100]{1,0:T(1,128)S(1)} %bitcast.8, f32[1,512]{1,0:T(1,128)S(1)} %bitcast.7, ...), custom_call_target="tpu_custom_call" | custom-call | flops 400000000 | bytes 4194304 | tf_op jit(solution)/shard_map/crps/pallas_call | solution.py:445
  66.3 23.1 %all_to_all.10.parts_ref = bf16[128,8,128]{2,1,0:T(8,128)(2,1)S(1)} all-to-all(bf16[128,8,128]{2,1,0:T(8,128)(2,1)S(1)} %get-tuple-element.24), channel_id=1, replica_groups=mesh['mem'=4,'lat'=32] {'mem','lat'}, dimensions={0} | all-to-all | bytes 524288 | tf_op jit(solution)/shard_map/all_to_all | solution.py:527
  89.4 0.9 share.1
  90.2 3.9 %all-to-all-start.1 = ((bf16[128,8,128]{2,1,0:T(8,128)(2,1)}), bf16[128,8,128]{2,1,0:T(8,128)(2,1)S(1)}, u32[]{:S(2)}, u32[]{:S(2)}) async-start(bf16[128,8,128]{2,1,0:T(8,128)(2,1)} %share.1), calls=%async_computation.1 | async-start | bytes 524288 | tf_op jit(solution)/shard_map/all_to_all | solution.py:536
  94.2 0.0 copy-done
  94.2 2.8 %backward.1 = bf16[2,512,1024]{2,1,0:T(8,128)(2,1)} custom-call(bf16[2,104,512]{2,1,0:T(8,128)(2,1)S(1)} %get-tuple-element.20.grad_ref, bf16[104,1024]{1,0:T(8,128)(2,1)S(1)} %get-tuple-element.21.dec_ref, bf16[2,512,1024]{2,1,0:T(8,128)(2,1)S(1)} %copy-done, f32[2,512,128]{2,1,0:T(8,128)S(1)} %get-tuple-element.23.inverse_ref), custom_call_target="tpu_custom_call" | custom-call | flops 500000000 | bytes 5242880 | tf_op jit(solution)/shard_map/backward/pallas_call | solution.py:480
  97.0 8.5 %all-to-all-done.1.pieces_ref = bf16[128,8,128]{2,1,0:T(8,128)(2,1)S(1)} async-done(((bf16[128,8,128]{2,1,0:T(8,128)(2,1)}), bf16[128,8,128]{2,1,0:T(8,128)(2,1)S(1)}, u32[]{:S(2)}, u32[]{:S(2)}) %all-to-all-start.1) | async-done | bytes 262176 | tf_op jit(solution)/shard_map/all_to_all | solution.py:536
  105.5 0.8 finish.1
Async XLA Ops:
  2.4 29.4 %collective-permute-start.1 = (bf16[2,256,1024]{2,1,0:T(8,128)(2,1)S(1)}, bf16[2,256,1024]{2,1,0:T(8,128)(2,1)}, u32[]{:S(2)}, u32[]{:S(2)}) collective-permute-start(bf16[2,256,1024]{2,1,0:T(8,128)(2,1)S(1)} %get-tuple-element.27), channel_id=1, source_target_pairs={{0,1},{1,2},{2,3},{3,4},{4,5},{5,6},{6,7},{7,8},{8,9},{9,10},{10,1... | collective-permute-start | bytes 3145736 | tf_op jit(solution)/shard_map/ppermute | solution.py:567
  7.4 25.6 %collective-permute-start = (bf16[2,256,1024]{2,1,0:T(8,128)(2,1)S(1)}, bf16[2,256,1024]{2,1,0:T(8,128)(2,1)S(1)}, u32[]{:S(2)}, u32[]{:S(2)}) collective-permute-start(bf16[2,256,1024]{2,1,0:T(8,128)(2,1)S(1)} %get-tuple-element.28), channel_id=1, source_target_pairs={{1,0},{2,1},{3,2},{4,3},{5,4},{6,5},{7,6},{8,7},{9,8},{10,9},{11,1... | collective-permute-start | bytes 3145736 | tf_op jit(solution)/shard_map/ppermute | solution.py:568
  8.7 24.3 %copy-start.3 = (s32[32]{0:T(128)S(1)}, s32[32]{0:T(128)}, u32[]{:S(2)}) copy-start(s32[32]{0:T(128)} %count_ref.5) | copy-start | bytes 388
  8.7 24.3 %copy-start.5 = (bf16[100,1024]{1,0:T(8,128)(2,1)S(1)}, bf16[100,1024]{1,0:T(8,128)(2,1)}, u32[]{:S(2)}) copy-start(bf16[100,1024]{1,0:T(8,128)(2,1)} %dec_ref.1) | copy-start | bytes 614404
  8.7 24.3 %copy-start.6 = (bf16[2,1024]{1,0:T(2,128)(2,1)S(1)}, bf16[2,1024]{1,0:T(2,128)(2,1)}, u32[]{:S(2)}) copy-start(bf16[2,1024]{1,0:T(2,128)(2,1)} %noise_ref.1) | copy-start | bytes 12292
  8.7 24.3 %copy-start.7 = (s32[1,2]{1,0:T(1,128)S(1)}, s32[1,2]{1,0:T(1,128)}, u32[]{:S(2)}) copy-start(s32[1,2]{1,0:T(1,128)} %window_ref.3) | copy-start | bytes 28
  33.0 30.6 %copy-start.1 = (f32[100,512]{1,0:T(8,128)S(1)}, f32[100,512]{1,0:T(8,128)}, u32[]{:S(2)}) copy-start(f32[100,512]{1,0:T(8,128)} %target_ref.1) | copy-start | bytes 614404
  33.0 30.6 %copy-start.2 = (f32[512]{0:T(512)S(1)}, f32[512]{0:T(512)}, u32[]{:S(2)}) copy-start(f32[512]{0:T(512)} %param.16) | copy-start | bytes 6148
  33.0 30.6 %copy-start.4 = (f32[100]{0:T(128)S(1)}, f32[100]{0:T(128)}, u32[]{:S(2)}) copy-start(f32[100]{0:T(128)} %param.17) | copy-start | bytes 1204
  63.6 30.5 %copy-start = (bf16[2,512,1024]{2,1,0:T(8,128)(2,1)S(1)}, bf16[2,512,1024]{2,1,0:T(8,128)(2,1)}, u32[]{:S(2)}) copy-start(bf16[2,512,1024]{2,1,0:T(8,128)(2,1)} %get-tuple-element.22.normalized_ref) | copy-start | bytes 6291460
  90.2 15.2 %all-to-all-start.1 = ((bf16[128,8,128]{2,1,0:T(8,128)(2,1)}), bf16[128,8,128]{2,1,0:T(8,128)(2,1)S(1)}, u32[]{:S(2)}, u32[]{:S(2)}) async-start(bf16[128,8,128]{2,1,0:T(8,128)(2,1)} %share.1), calls=%async_computation.1 | async-start | bytes 524288 | tf_op jit(solution)/shard_map/all_to_all | solution.py:536
